TPU v7x, 32 devices: a whole 2x2x4 slice. The times are simulated.
32 devices in a mesh: page: 8 (over z, y), seq: 4 (over x, core).
Axes of the slice: x: 2, y: 2, z: 4, core: 2. Of those that a mesh axis runs over, the one named last changes fastest.
Arguments:
- tokens: bfloat16 [24, 512, 768], P('page', 'seq'), may hold values from -6 to 6
- patches: bfloat16 [24, 64, 768], P('page', 'seq'), may hold values from -6 to 6
- page_length: int32 [24], P('page'), may hold values from 64 to 512, as said below
- box_position: int32 [2, 24, 512], P(None, 'page'), may hold values from 0 to 1023
- query_weight: bfloat16 [768, 768], replicated, may hold values from -0.21875 to 0.21875
- key_weight: bfloat16 [768, 768], replicated, may hold values from -0.21875 to 0.21875
- value_weight: bfloat16 [768, 768], replicated, may hold values from -0.21875 to 0.21875
- out_weight: bfloat16 [768, 768], replicated, may hold values from -0.625 to 0.625
- up_weight: bfloat16 [768, 3072], replicated, may hold values from -0.21875 to 0.21875
- down_weight: bfloat16 [3072, 768], replicated, may hold values from -0.109375 to 0.109375
- conv_weight: bfloat16 [768, 9], replicated, may hold values from -1.796875 to 1.796875
- patch_conv_weight: bfloat16 [768, 9], replicated, may hold values from -1.796875 to 1.796875
- query_bias: bfloat16 [768], replicated, may hold values from -3 to 3
- value_bias: bfloat16 [768], replicated, may hold values from -3 to 3
- out_bias: bfloat16 [768], replicated, may hold values from -3 to 3
- up_bias: bfloat16 [3072], replicated, may hold values from -3 to 3
- down_bias: bfloat16 [768], replicated, may hold values from -3 to 3
- attention_gain: bfloat16 [768], replicated, may hold values from 0.5 to 1.5
- attention_shift: bfloat16 [768], replicated, may hold values from -1.796875 to 1.796875
- feedforward_gain: bfloat16 [768], replicated, may hold values from 0.5 to 1.5
- feedforward_shift: bfloat16 [768], replicated, may hold values from -1.796875 to 1.796875
- reading_bias_table: bfloat16 [12, 32], replicated, may hold values from -4 to 4
- horizontal_bias_table: bfloat16 [12, 64], replicated, may hold values from -4 to 4
- vertical_bias_table: bfloat16 [12, 64], replicated, may hold values from -4 to 4
- cotangent: bfloat16 [24, 512, 768], P('page', 'seq'), may hold values from -6 to 6
- patch_cotangent: bfloat16 [24, 64, 768], P('page', 'seq'), may hold values from -6 to 6
Outputs:
- output: float32 [24, 512, 768], P('page', 'seq')
- patch_output: float32 [24, 64, 768], P('page', 'seq')
- tokens_gradient: float32 [24, 512, 768], P('page', 'seq')
- patches_gradient: float32 [24, 64, 768], P('page', 'seq')
- query_weight_gradient: float32 [768, 768], P('page', 'seq')
- key_weight_gradient: float32 [768, 768], P('page', 'seq')
- value_weight_gradient: float32 [768, 768], P('page', 'seq')
- out_weight_gradient: float32 [768, 768], P('page', 'seq')
- up_weight_gradient: float32 [768, 3072], P('page', 'seq')
- down_weight_gradient: float32 [3072, 768], P('page', 'seq')
- conv_weight_gradient: float32 [768, 9], replicated
- patch_conv_weight_gradient: float32 [768, 9], replicated
- query_bias_gradient: float32 [768], replicated
- value_bias_gradient: float32 [768], replicated
- out_bias_gradient: float32 [768], replicated
- up_bias_gradient: float32 [3072], replicated
- down_bias_gradient: float32 [768], replicated
- attention_gain_gradient: float32 [768], replicated
- attention_shift_gradient: float32 [768], replicated
- feedforward_gain_gradient: float32 [768], replicated
- feedforward_shift_gradient: float32 [768], replicated
- line_table_gradient: float32 [12, 32], replicated
- across_table_gradient: float32 [12, 64], replicated
- upward_table_gradient: float32 [12, 64], replicated
Inputs may be any that keep to these rules, and one draw needn't show every extreme that they name: `page_length`: in every aligned block of 3 pages (the pages of one index of page) at least one page has 512 tokens.
All inputs are finite; a program needn't handle non-finite values.
Results may differ from a plain program's by a relative error of at most 0.019.
The roundings to bfloat16 on the way count: a program that leaves them out, or rounds other values in their place, can miss the bound.
Values may be sent and summed in bfloat16 or wider, within the bound.
A program may use at most 256 MiB of HBM per device.

v0:
```python
import jax
import jax.numpy as jnp
from jax import lax
from jax.sharding import PartitionSpec as P

GRID_SIDE = 8


epsilon = 1e-05
coordinate_step = 16
masked_score = -1000000000.0
patch_pitch = 146
patch_centre = 73


def with_halo(cells, sides, width):
    for axis, dim in sides:
        count = lax.axis_size(axis)
        ends = count - 1
        head = lax.slice_in_dim(cells, 0, width, axis=dim)
        tail = lax.slice_in_dim(cells, cells.shape[dim] - width, cells.shape[dim], axis=dim)
        cells = jnp.concatenate(
            [
                lax.ppermute(tail, axis, [(i, (i + 1) % count) for i in range(ends)]),
                cells,
                lax.ppermute(head, axis, [((i + 1) % count, i) for i in range(ends)]),
            ],
            axis=dim,
        )
    return cells


def layer_norm(values, gain_vector, shift_vector):
    row_mean = jnp.mean(values, axis=-1, keepdims=True)
    centred = values - row_mean
    variance = jnp.mean(centred * centred, axis=-1, keepdims=True)
    return centred * lax.rsqrt(variance + epsilon) * gain_vector + shift_vector


def gelu_exact(values):
    return jax.nn.gelu(values, approximate=False)


def flat_dot(operand, matrix):
    front = operand.shape[:-1]
    result = jnp.dot(
        operand.reshape(-1, operand.shape[-1]), matrix, preferred_element_type=jnp.float32
    )
    return result.reshape(front + (matrix.shape[-1],))


def back_dot(operand, matrix):
    front = operand.shape[:-1]
    result = lax.dot_general(
        operand.reshape(-1, operand.shape[-1]),
        matrix,
        (((1,), (1,)), ((), ())),
        preferred_element_type=jnp.float32,
    )
    return result.reshape(front + (matrix.shape[0],))


def outer_dot(operand, gradient):
    return lax.dot_general(
        operand.reshape(-1, operand.shape[-1]),
        gradient.reshape(-1, gradient.shape[-1]),
        (((0,), (0,)), ((), ())),
        preferred_element_type=jnp.float32,
    )


def row_sum(gradient):
    return jnp.sum(gradient.astype(jnp.float32).reshape(-1, gradient.shape[-1]), axis=0)


def plane_hots(query_coord, key_coord, bins):
    half_bins = bins // 2
    bucket = (
        jnp.clip(
            jnp.floor_divide(key_coord[None, :] - query_coord[:, None], coordinate_step),
            -half_bins,
            half_bins - 1,
        )
        + half_bins
    )
    return (bucket[None, :, :] == jnp.arange(bins, dtype=jnp.int32)[:, None, None]).astype(
        jnp.bfloat16
    )


def grid_live(cells):
    return (cells // GRID_SIDE < GRID_SIDE - 1) & (cells % GRID_SIDE < GRID_SIDE - 1)


def grid_boxes(cells):
    return jnp.stack(
        [
            patch_pitch * (cells % GRID_SIDE) + patch_centre,
            patch_pitch * (cells // GRID_SIDE) + patch_centre,
        ]
    )


def shards(
    tokens,
    patches,
    page_length,
    box_position,
    query_weight,
    key_weight,
    value_weight,
    out_weight,
    up_weight,
    down_weight,
    conv_weight,
    patch_conv_weight,
    query_bias,
    value_bias,
    out_bias,
    up_bias,
    down_bias,
    attention_gain,
    attention_shift,
    feedforward_gain,
    feedforward_shift,
    reading_bias_table,
    horizontal_bias_table,
    vertical_bias_table,
    cotangent,
    patch_cotangent,
):
    conv_taps = conv_weight.astype(jnp.float32)
    patch_taps = patch_conv_weight.astype(jnp.float32)
    query_offset = query_bias.astype(jnp.float32)
    value_offset = value_bias.astype(jnp.float32)
    out_offset = out_bias.astype(jnp.float32)
    up_offset = up_bias.astype(jnp.float32)
    down_offset = down_bias.astype(jnp.float32)
    first_gain = attention_gain.astype(jnp.float32)
    first_shift = attention_shift.astype(jnp.float32)
    second_gain = feedforward_gain.astype(jnp.float32)
    second_shift = feedforward_shift.astype(jnp.float32)
    page_count, span_size, model_width = tokens.shape
    patch_span = patches.shape[1]
    seq_count = lax.axis_size("seq")
    slot_size = span_size * seq_count
    patch_slots = patch_span * seq_count
    row_count = span_size + patch_span
    key_count = row_count * seq_count
    head_count = reading_bias_table.shape[0]
    head_size = model_width // head_count
    line_bins = reading_bias_table.shape[1]
    plane_bins = horizontal_bias_table.shape[1]
    score_scale = head_size ** (-0.5)
    seq_index = lax.axis_index("seq")
    text_places = seq_index * span_size + jnp.arange(span_size, dtype=jnp.int32)
    local_cells = seq_index * patch_span + jnp.arange(patch_span, dtype=jnp.int32)
    query_places = jnp.concatenate([text_places, slot_size + local_cells])
    all_cells = jnp.arange(patch_slots, dtype=jnp.int32)
    key_places = jnp.concatenate(
        [
            jnp.arange(slot_size, dtype=jnp.int32).reshape(seq_count, span_size),
            (slot_size + all_cells).reshape(seq_count, patch_span),
        ],
        axis=1,
    ).reshape(key_count)
    text_live = text_places[None, :] < page_length[:, None]
    patch_live = grid_live(local_cells)
    all_text_live = (
        jnp.arange(slot_size, dtype=jnp.int32)[None, :] < page_length[:, None]
    ).reshape(page_count, seq_count, span_size)
    all_patch_live = jnp.broadcast_to(
        grid_live(all_cells).reshape(1, seq_count, patch_span), (page_count, seq_count, patch_span)
    )
    key_mask = jnp.concatenate([all_text_live, all_patch_live], axis=2).reshape(
        page_count, key_count
    )
    text_box_all = box_position.reshape(2, page_count, seq_count, span_size)
    patch_box_all = jnp.broadcast_to(
        grid_boxes(all_cells).reshape(2, 1, seq_count, patch_span),
        (2, page_count, seq_count, patch_span),
    )
    key_box = jnp.concatenate([text_box_all, patch_box_all], axis=3).reshape(
        2, page_count, key_count
    )
    local_patch_box = jnp.broadcast_to(
        grid_boxes(local_cells)[:, None, :], (2, page_count, patch_span)
    )
    query_box = jnp.concatenate(
        [
            lax.dynamic_slice_in_dim(box_position, seq_index * span_size, span_size, 2),
            local_patch_box,
        ],
        axis=2,
    )
    text_factor = text_live[:, :, None]
    patch_factor = patch_live[None, :, None]
    masked = tokens * text_factor.astype(jnp.bfloat16)
    rimmed = with_halo(masked, (("seq", 1),), 3)
    convolved = jnp.zeros((page_count, span_size, model_width), jnp.float32)
    for dilation in (1, 2, 3):
        for offset in (-1, 0, 1):
            column = 3 * (dilation - 1) + offset + 1
            anchor = 3 + offset * dilation
            convolved = convolved + rimmed[:, anchor : anchor + span_size, :] * conv_taps[:, column]
    reach = GRID_SIDE + 1
    patch_masked = patches * patch_factor.astype(jnp.bfloat16)
    patch_rimmed = with_halo(patch_masked, (("seq", 1),), reach)
    patch_convolved = jnp.zeros((page_count, patch_span, model_width), jnp.float32)
    for vertical in (-1, 0, 1):
        for horizontal in (-1, 0, 1):
            column = 3 * (vertical + 1) + horizontal + 1
            anchor = reach + vertical * GRID_SIDE + horizontal
            patch_convolved = (
                patch_convolved
                + patch_rimmed[:, anchor : anchor + patch_span, :] * patch_taps[:, column]
            )
    hidden = jnp.concatenate(
        [tokens.astype(jnp.float32) + convolved, patches.astype(jnp.float32) + patch_convolved],
        axis=1,
    )
    hidden_low = hidden.astype(jnp.bfloat16)
    queries = (flat_dot(hidden_low, query_weight) + query_offset).astype(jnp.bfloat16)
    key_rows = flat_dot(hidden_low, key_weight).astype(jnp.bfloat16)
    value_rows = (flat_dot(hidden_low, value_weight) + value_offset).astype(jnp.bfloat16)
    key_all, value_all = (
        lax.all_gather(key_rows, "seq", axis=1, tiled=True),
        lax.all_gather(value_rows, "seq", axis=1, tiled=True),
    )
    half_line = line_bins // 2
    line_bucket = (
        jnp.clip(key_places[None, :] - query_places[:, None], -half_line, half_line - 1) + half_line
    )
    reading_onehot = (
        line_bucket[None, :, :] == jnp.arange(line_bins, dtype=jnp.int32)[:, None, None]
    ).astype(jnp.bfloat16)
    reading_bias_part = jnp.einsum(
        "cd,dof->cof", reading_bias_table, reading_onehot, preferred_element_type=jnp.float32
    )
    query_pages = jnp.moveaxis(query_box, 1, 0)
    key_pages = jnp.moveaxis(key_box, 1, 0)

    def page_bias(page_inputs):
        query_page, key_page = page_inputs
        horizontal_onehot = plane_hots(query_page[0], key_page[0], plane_bins)
        vertical_onehot = plane_hots(query_page[1], key_page[1], plane_bins)
        across_part = jnp.einsum(
            "cd,dof->cof",
            horizontal_bias_table,
            horizontal_onehot,
            preferred_element_type=jnp.float32,
        )
        upward_part = jnp.einsum(
            "cd,dof->cof", vertical_bias_table, vertical_onehot, preferred_element_type=jnp.float32
        )
        return across_part + upward_part

    bias = reading_bias_part[None] + lax.map(page_bias, (query_pages, key_pages))
    query_heads = queries.reshape(page_count, row_count, head_count, head_size)

    def attention_scores(key_source):
        key_heads = key_source.reshape(page_count, key_count, head_count, head_size)
        scores = (
            jnp.einsum(
                "pqhe,pkhe->phqk", query_heads, key_heads, preferred_element_type=jnp.float32
            )
            * score_scale
            + bias
        )
        return jnp.where(key_mask[:, None, None, :], scores, masked_score)

    scores = attention_scores(key_all)
    row_max = jnp.max(scores, axis=-1, keepdims=True)
    shifted_exp = jnp.exp(scores - row_max)
    row_total = jnp.sum(shifted_exp, axis=-1, keepdims=True)
    log_total = row_max + jnp.log(row_total)
    weights_low = (shifted_exp / row_total).astype(jnp.bfloat16)
    value_heads = value_all.reshape(page_count, key_count, head_count, head_size)
    mixture = jnp.einsum(
        "phqk,pkhe->pqhe", weights_low, value_heads, preferred_element_type=jnp.float32
    )
    mixture_low = mixture.reshape(page_count, row_count, model_width).astype(jnp.bfloat16)
    attention = flat_dot(mixture_low, out_weight) + out_offset
    first_input = hidden + attention
    normed = layer_norm(first_input, first_gain, first_shift)
    normed_low = normed.astype(jnp.bfloat16)
    up_branch = flat_dot(normed_low, up_weight) + up_offset
    activated_low = gelu_exact(up_branch).astype(jnp.bfloat16)
    down_branch = flat_dot(activated_low, down_weight) + down_offset
    second_input = normed + down_branch
    output = layer_norm(second_input, second_gain, second_shift)
    delta_output = jnp.concatenate([cotangent, patch_cotangent], axis=1).astype(jnp.float32)
    second_pullback = jax.vjp(layer_norm, second_input, second_gain, second_shift)[1]
    delta_second, delta_second_gain, delta_second_shift = second_pullback(delta_output)
    delta_down = delta_second.astype(jnp.bfloat16)
    delta_down_offset = row_sum(delta_down)
    delta_down_matrix = outer_dot(activated_low, delta_down)
    delta_activated = back_dot(delta_down, down_weight)
    delta_up = jax.vjp(gelu_exact, up_branch)[1](delta_activated)[0].astype(jnp.bfloat16)
    delta_up_offset = row_sum(delta_up)
    delta_up_matrix = outer_dot(normed_low, delta_up)
    delta_normed = delta_second + back_dot(delta_up, up_weight)
    first_pullback = jax.vjp(layer_norm, first_input, first_gain, first_shift)[1]
    delta_first, delta_first_gain, delta_first_shift = first_pullback(delta_normed)
    delta_attention = delta_first.astype(jnp.bfloat16)
    delta_out_offset = row_sum(delta_attention)
    delta_out_matrix = outer_dot(mixture_low, delta_attention)
    delta_mixture = back_dot(delta_attention, out_weight).astype(jnp.bfloat16)
    key_back, value_back = (
        lax.all_gather(key_rows, "seq", axis=1, tiled=True),
        lax.all_gather(value_rows, "seq", axis=1, tiled=True),
    )
    key_back_heads = key_back.reshape(page_count, key_count, head_count, head_size)
    value_back_heads = value_back.reshape(page_count, key_count, head_count, head_size)
    weights_again = jnp.exp(attention_scores(key_back) - log_total)
    weights_again_low = weights_again.astype(jnp.bfloat16)
    delta_heads = delta_mixture.reshape(page_count, row_count, head_count, head_size)
    delta_weights = jnp.einsum(
        "pqhe,pkhe->phqk", delta_heads, value_back_heads, preferred_element_type=jnp.float32
    )
    scores_gradient = (
        weights_again
        * (delta_weights - jnp.sum(weights_again * delta_weights, axis=-1, keepdims=True))
    ).astype(jnp.bfloat16)
    delta_queries = (
        (
            jnp.einsum(
                "phqk,pkhe->pqhe",
                scores_gradient,
                key_back_heads,
                preferred_element_type=jnp.float32,
            )
            * score_scale
        )
        .reshape(page_count, row_count, model_width)
        .astype(jnp.bfloat16)
    )
    delta_key_all = (
        jnp.einsum(
            "phqk,pqhe->pkhe", scores_gradient, query_heads, preferred_element_type=jnp.float32
        )
        * score_scale
    ).reshape(page_count, key_count, model_width)
    delta_value_all = jnp.einsum(
        "phqk,pqhe->pkhe", weights_again_low, delta_heads, preferred_element_type=jnp.float32
    ).reshape(page_count, key_count, model_width)
    delta_key_sum, delta_value_sum = (
        lax.psum_scatter(
            delta_key_all.astype(jnp.bfloat16), "seq", scatter_dimension=1, tiled=True
        ).astype(jnp.float32),
        lax.psum_scatter(
            delta_value_all.astype(jnp.bfloat16), "seq", scatter_dimension=1, tiled=True
        ).astype(jnp.float32),
    )
    delta_keys = delta_key_sum.astype(jnp.bfloat16)
    delta_values = delta_value_sum.astype(jnp.bfloat16)
    delta_line = jnp.einsum(
        "aiey,jey->ij", scores_gradient, reading_onehot, preferred_element_type=jnp.float32
    )

    def page_delta(page_inputs):
        page_gradient_rows, query_page, key_page = page_inputs
        horizontal_onehot = plane_hots(query_page[0], key_page[0], plane_bins)
        vertical_onehot = plane_hots(query_page[1], key_page[1], plane_bins)
        across_sum = jnp.einsum(
            "iwu,twu->it", page_gradient_rows, horizontal_onehot, preferred_element_type=jnp.float32
        )
        upward_sum = jnp.einsum(
            "iwu,twu->it", page_gradient_rows, vertical_onehot, preferred_element_type=jnp.float32
        )
        return (across_sum, upward_sum)

    across_parts, upward_parts = lax.map(page_delta, (scores_gradient, query_pages, key_pages))
    delta_across = jnp.sum(across_parts, axis=0)
    delta_upward = jnp.sum(upward_parts, axis=0)
    delta_query_offset = row_sum(delta_queries)
    delta_value_offset = row_sum(delta_values)
    delta_query_matrix = outer_dot(hidden_low, delta_queries)
    delta_key_matrix = outer_dot(hidden_low, delta_keys)
    delta_value_matrix = outer_dot(hidden_low, delta_values)
    delta_hidden = (
        delta_first
        + back_dot(delta_queries, query_weight)
        + back_dot(delta_keys, key_weight)
        + back_dot(delta_values, value_weight)
    )
    delta_position = delta_hidden[:, :span_size].astype(jnp.bfloat16)
    delta_rim = with_halo(delta_position, (("seq", 1),), 3)
    delta_masked = jnp.zeros((page_count, span_size, model_width), jnp.float32)
    tap_columns = []
    for dilation in (1, 2, 3):
        for offset in (-1, 0, 1):
            column = 3 * (dilation - 1) + offset + 1
            anchor = 3 + offset * dilation
            anchor_back = 3 - offset * dilation
            delta_masked = (
                delta_masked
                + delta_rim[:, anchor_back : anchor_back + span_size, :] * conv_taps[:, column]
            )
            tap_columns.append(
                jnp.einsum(
                    "ptd,ptd->d",
                    delta_position,
                    rimmed[:, anchor : anchor + span_size, :],
                    preferred_element_type=jnp.float32,
                )
            )
    delta_taps = jnp.stack(tap_columns, axis=1)
    tokens_gradient = delta_hidden[:, :span_size] + delta_masked * text_factor.astype(jnp.float32)
    delta_patch_position = delta_hidden[:, span_size:].astype(jnp.bfloat16)
    delta_patch_rim = with_halo(delta_patch_position, (("seq", 1),), reach)
    delta_patch_masked = jnp.zeros((page_count, patch_span, model_width), jnp.float32)
    patch_columns = []
    for vertical in (-1, 0, 1):
        for horizontal in (-1, 0, 1):
            column = 3 * (vertical + 1) + horizontal + 1
            anchor = reach + vertical * GRID_SIDE + horizontal
            anchor_back = reach - vertical * GRID_SIDE - horizontal
            delta_patch_masked = (
                delta_patch_masked
                + delta_patch_rim[:, anchor_back : anchor_back + patch_span, :]
                * patch_taps[:, column]
            )
            patch_columns.append(
                jnp.einsum(
                    "ptd,ptd->d",
                    delta_patch_position,
                    patch_rimmed[:, anchor : anchor + patch_span, :],
                    preferred_element_type=jnp.float32,
                )
            )
    delta_patch_taps = jnp.stack(patch_columns, axis=1)
    patches_gradient = delta_hidden[:, span_size:] + delta_patch_masked * patch_factor.astype(
        jnp.float32
    )
    matrix_rows = (
        lax.psum_scatter(delta_query_matrix, "page", scatter_dimension=0, tiled=True),
        lax.psum_scatter(delta_key_matrix, "page", scatter_dimension=0, tiled=True),
        lax.psum_scatter(delta_value_matrix, "page", scatter_dimension=0, tiled=True),
        lax.psum_scatter(delta_out_matrix, "page", scatter_dimension=0, tiled=True),
        lax.psum_scatter(delta_up_matrix, "page", scatter_dimension=0, tiled=True),
        lax.psum_scatter(delta_down_matrix, "page", scatter_dimension=0, tiled=True),
    )
    matrix_parts = (
        lax.psum_scatter(
            matrix_rows[0].astype(jnp.bfloat16), "seq", scatter_dimension=1, tiled=True
        ).astype(jnp.float32),
        lax.psum_scatter(
            matrix_rows[1].astype(jnp.bfloat16), "seq", scatter_dimension=1, tiled=True
        ).astype(jnp.float32),
        lax.psum_scatter(
            matrix_rows[2].astype(jnp.bfloat16), "seq", scatter_dimension=1, tiled=True
        ).astype(jnp.float32),
        lax.psum_scatter(
            matrix_rows[3].astype(jnp.bfloat16), "seq", scatter_dimension=1, tiled=True
        ).astype(jnp.float32),
        lax.psum_scatter(
            matrix_rows[4].astype(jnp.bfloat16), "seq", scatter_dimension=1, tiled=True
        ).astype(jnp.float32),
        lax.psum_scatter(
            matrix_rows[5].astype(jnp.bfloat16), "seq", scatter_dimension=1, tiled=True
        ).astype(jnp.float32),
    )
    vector_parts = lax.psum(
        (
            delta_taps,
            delta_patch_taps,
            delta_query_offset,
            delta_value_offset,
            delta_out_offset,
            delta_up_offset,
            delta_down_offset,
            delta_first_gain,
            delta_first_shift,
            delta_second_gain,
            delta_second_shift,
            delta_line,
            delta_across,
            delta_upward,
        ),
        ("page", "seq"),
    )
    return (
        output[:, :span_size],
        output[:, span_size:],
        tokens_gradient,
        patches_gradient,
        matrix_parts[0],
        matrix_parts[1],
        matrix_parts[2],
        matrix_parts[3],
        matrix_parts[4],
        matrix_parts[5],
        vector_parts[0],
        vector_parts[1],
        vector_parts[2],
        vector_parts[3],
        vector_parts[4],
        vector_parts[5],
        vector_parts[6],
        vector_parts[7],
        vector_parts[8],
        vector_parts[9],
        vector_parts[10],
        vector_parts[11],
        vector_parts[12],
        vector_parts[13],
    )


def solution(mesh):
    in_specs = (
        P("page", "seq", None),
        P("page", "seq", None),
        P("page"),
        P(None, "page", None),
        P(),
        P(),
        P(),
        P(),
        P(),
        P(),
        P(),
        P(),
        P(),
        P(),
        P(),
        P(),
        P(),
        P(),
        P(),
        P(),
        P(),
        P(),
        P(),
        P(),
        P("page", "seq", None),
        P("page", "seq", None),
    )
    out_specs = (
        P("page", "seq", None),
        P("page", "seq", None),
        P("page", "seq", None),
        P("page", "seq", None),
        P("page", "seq"),
        P("page", "seq"),
        P("page", "seq"),
        P("page", "seq"),
        P("page", "seq"),
        P("page", "seq"),
        P(),
        P(),
        P(),
        P(),
        P(),
        P(),
        P(),
        P(),
        P(),
        P(),
        P(),
        P(),
        P(),
        P(),
    )
    return jax.shard_map(shards, mesh=mesh, in_specs=in_specs, out_specs=out_specs, check_vma=False)
```

profile of v0, /device:TPU:0, one launch (start us, length us, event | category | flops | bytes accessed | tf_op | source)
XLA Modules:
  0.0 1176.5 jit_solution(3356589348554042150)
XLA Ops:
  28.1 34.2 %while.28 = (s32[]{:T(128)}, f32[3,12,144,576]{3,2,1,0:T(8,128)}, s32[3,2,576]{2,1,0:T(2,128)S(1)}, s32[3,2,144]{2,1,0:T(2,128)S(1)}, bf16[12,64]{1,0:T(8,128)(2...) while((s32[]{:T(128)}, f32[3,12,144,576]{3,2,1,0:T(8,128)}, ...), condition=%wide.region_1.2_spmd, body=%wide.region_0.1_spmd.sunk | while | flops 269402112 | bytes 21696516 | solution.py:258
  73.2 5.5 copy.84
  78.7 15.7 %fusion.194 = (f32[3,12,144]{2,1,0:T(8,128)S(1)}, f32[3,12,144,576]{3,2,1,0:T(8,128)}) fusion(f32[3,12,144,576]{3,2,1,0:T(8,128)} %get-tuple-element.221, f32[12,144,576]{2,1,0:T(8,128)} %copy.85, bf16[3,144,12,64]{1,3,2,0:T(8,128)(2,1)S(1)} %bitcast.267, bf16[3,576,12,64]{1,3,2,0:T(8,128)(2,1)} %bitcast.260, pred[3,576]{1,0:T(4,128)(4,1)S(1)} %broadcast_in_dim.63), kind=kOutput, calls=%fused_computation.417 | convolution fusion | flops 397130688 | bytes 31209408 | tf_op jit(solution)/shard_map/pqhe,pkhe->phqk/dot_general | solution.py:264
  94.4 6.6 fusion.44
  101.1 5.4 copy.82
  106.5 7.4 fusion.75
  115.3 7.1 fusion.92
  122.4 12.4 %multiply_convert_fusion.2 = (bf16[3,144,3072]{2,1,0:T(8,128)(2,1)S(1)}, f32[3,144,3072]{2,1,0:T(8,128)S(1)}) fusion(f32[3,144,3072]{2,1,0:T(8,128)S(1)} %get-tuple-element.444, f32[3072]{0:T(1024)S(1)} %convert_element_type.368, u8[144,3072]{1,0:T(8,128)(4,1)S(1)} %get-tuple-element.319, u8[144,3072]{1,0:T(8,128)(4,1)S(1)} %get-tuple-element.318), kind=kLoop, calls=%fused_computation.116 | loop fusion | flops 94224384 | bytes 14168064 | tf_op jit(solution)/shard_map/convert_element_type | solution.py:288
  141.5 8.5 convert_reduce_fusion.1
  150.0 6.6 multiply_reduce_fusion.1
  162.1 7.6 fusion.70
  169.7 5.3 copy.91
  175.1 7.9 multiply_reduce_fusion
  183.0 9.5 convert_reduce_fusion
  196.2 5.3 copy.90
  205.4 6.7 convert_reduce_fusion.2
  218.2 31.8 %reduce-scatter.25.cloned.1.call-done = bf16[3,144,768]{2,1,0:T(8,128)(2,1)} async-done(((bf16[3,576,768]{2,1,0:T(8,128)(2,1)}), bf16[3,144,768]{2,1,0:T(8,128)(2,1)}) %reduce-scatter.25.cloned.1.call-update) | async-done | bytes 663568 | tf_op jit(solution)/shard_map/reduce_scatter | solution.py:348
  254.3 8.1 convolution_bitcast_fusion
  262.4 59.8 %reduce-scatter.35.cloned.1.call-done = f32[96,768]{1,0:T(8,128)} async-done(((f32[768,768]{1,0:T(8,128)}), f32[96,768]{1,0:T(8,128)}) %reduce-scatter.35.cloned.1.call-update) | async-done | bytes 294928 | tf_op jit(solution)/shard_map/reduce_scatter | solution.py:440
  324.2 69.7 %reduce-scatter.29.cloned.1.call-done = f32[96,768]{1,0:T(8,128)} async-done(((f32[768,768]{1,0:T(8,128)}), f32[96,768]{1,0:T(8,128)}) %reduce-scatter.29.cloned.1.call-update) | async-done | bytes 294928 | tf_op jit(solution)/shard_map/reduce_scatter | solution.py:437
  395.8 8.7 convolution_bitcast_fusion.1
  404.5 61.0 %reduce-scatter.33.cloned.1.call-done = f32[96,768]{1,0:T(8,128)} async-done(((f32[768,768]{1,0:T(8,128)}), f32[96,768]{1,0:T(8,128)}) %reduce-scatter.33.cloned.1.call-update) | async-done | bytes 294928 | tf_op jit(solution)/shard_map/reduce_scatter | solution.py:439
  468.0 69.1 %reduce-scatter.31.cloned.1.call-done = f32[96,768]{1,0:T(8,128)} async-done(((f32[768,768]{1,0:T(8,128)}), f32[96,768]{1,0:T(8,128)}) %reduce-scatter.31.cloned.1.call-update) | async-done | bytes 294928 | tf_op jit(solution)/shard_map/reduce_scatter | solution.py:438
  539.0 35.7 %while.29 = (s32[]{:T(128)}, f32[3,12,64]{2,1,0:T(8,128)S(1)}, f32[3,12,64]{2,1,0:T(8,128)S(1)}, bf16[3,12,144,576]{3,2,1,0:T(8,128)(2,1)}, s32[3,2,576]{2,1,0:T...) while((s32[]{:T(128)}, f32[3,12,64]{2,1,0:T(8,128)S(1)}, f32[3,12,64]{2,1,0:T(8,128)S(1)}, ...), condition=%wide.region_50.51_spmd, body=%wide.region_49.50_spmd.sunk | while | flops 268406784 | bytes 9839629 | solution.py:373
  574.7 129.7 %reduce-scatter.41.cloned.1.call-done = f32[384,768]{1,0:T(8,128)} async-done(((f32[3072,768]{1,0:T(8,128)}), f32[384,768]{1,0:T(8,128)}) %reduce-scatter.41.cloned.1.call-update) | async-done | bytes 1179664 | tf_op jit(solution)/shard_map/reduce_scatter | solution.py:442
  715.3 10.8 reduce-scatter.49.cloned.1.call-done
  727.7 21.3 %reduce-scatter.43.cloned.1.call-done = bf16[192,96]{1,0:T(8,128)(2,1)} async-done(((bf16[768,96]{1,0:T(8,128)(2,1)}), bf16[192,96]{1,0:T(8,128)(2,1)}) %reduce-scatter.43.cloned.1.call-update) | async-done | bytes 36880
  754.4 161.3 %reduce-scatter.37.cloned.1.call-done = f32[96,3072]{1,0:T(8,128)} async-done(((f32[768,3072]{1,0:T(8,128)}), f32[96,3072]{1,0:T(8,128)}) %reduce-scatter.37.cloned.1.call-update) | async-done | bytes 1179664 | tf_op jit(solution)/shard_map/reduce_scatter | solution.py:441
  941.7 18.0 %reduce-scatter.45.cloned.1.call-done = bf16[192,96]{1,0:T(8,128)(2,1)} async-done(((bf16[768,96]{1,0:T(8,128)(2,1)}), bf16[192,96]{1,0:T(8,128)(2,1)}) %reduce-scatter.45.cloned.1.call-update) | async-done | bytes 36880
  961.3 22.9 %reduce-scatter.51.cloned.1.call-done = bf16[192,384]{1,0:T(8,128)(2,1)} async-done(((bf16[768,384]{1,0:T(8,128)(2,1)}), bf16[192,384]{1,0:T(8,128)(2,1)}) %reduce-scatter.51.cloned.1.call-update) | async-done | bytes 147472
  986.1 22.6 %reduce-scatter.39.cloned.1.call-done = bf16[96,768]{1,0:T(8,128)(2,1)} async-done(((bf16[96,3072]{1,0:T(8,128)(2,1)}), bf16[96,768]{1,0:T(8,128)(2,1)}) %reduce-scatter.39.cloned.1.call-update) | async-done | bytes 147472 | tf_op jit(solution)/shard_map/reduce_scatter | solution.py:457
  1010.3 141.2 %all-reduce.3.cloned.1.call-done = (f32[768,9]{0,1:T(8,128)}, f32[768,9]{0,1:T(8,128)}, f32[768]{0:T(1024)}, f32[768]{0:T(1024)}, f32[768]{0:T(1024)}, /*index=5...) async-done(((f32[768,9]{0,1:T(8,128)}, f32[768,9]{0,1:T(8,128)}, ...) | async-done | bytes 99856 | tf_op jit(solution)/shard_map/psum | solution.py:464
  (438 shorter events, 206.5 us)
Async XLA Ops:
  7.2 106.7 %copy-start = (bf16[768,768]{1,0:T(8,128)(2,1)S(1)}, bf16[768,768]{1,0:T(8,128)(2,1)}, u32[]{:S(2)}) copy-start(bf16[768,768]{1,0:T(8,128)(2,1)} %param.37) | copy-start | bytes 3538948
  7.3 65.9 %all-gather.5.cloned.1.call-start = ((), (), s32[]{:S(2)}) async-start(), calls=%async_computation.15 | async-start | bytes 3317760 | tf_op jit(solution)/shard_map/all_gather | solution.py:227
  8.5 16.0 %collective-permute-start.3 = (bf16[3,9,768]{2,1,0:T(8,128)(2,1)S(1)}, bf16[3,9,768]{2,1,0:T(8,128)(2,1)S(1)}, u32[]{:S(2)}, u32[]{:S(2)}) collective-permute-start(bf16[3,9,768]{2,1,0:T(8,128)(2,1)S(1)} %get-tuple-element.434), channel_id=1, source_target_pairs={{1,0},{2,1},{3,2},{5,4},{6,5},{7,6},{9,8},{10,9},{11,10},{13,12},{... | collective-permute-start | bytes 124424 | tf_op jit(solution)/shard_map/ppermute | solution.py:26
  9.8 14.8 %collective-permute-start.2 = (bf16[3,9,768]{2,1,0:T(8,128)(2,1)S(1)}, bf16[3,9,768]{2,1,0:T(8,128)(2,1)S(1)}, u32[]{:S(2)}, u32[]{:S(2)}) collective-permute-start(bf16[3,9,768]{2,1,0:T(8,128)(2,1)S(1)} %get-tuple-element.435), channel_id=1, source_target_pairs={{0,1},{1,2},{2,3},{4,5},{5,6},{6,7},{8,9},{9,10},{10,11},{12,13},{... | collective-permute-start | bytes 124424 | tf_op jit(solution)/shard_map/ppermute | solution.py:24
  15.4 6.7 collective-permute-start
  19.9 3.1 collective-permute-start.1
  26.3 43.8 %copy-start.28 = (bf16[3,144,768]{2,1,0:T(8,128)(2,1)}, bf16[3,144,768]{2,1,0:T(8,128)(2,1)S(1)}, u32[]{:S(2)}) copy-start(bf16[3,144,768]{2,1,0:T(8,128)(2,1)S(1)} %fusion.132) | copy-start | bytes 1990660
  27.9 73.2 %all-gather.3.cloned.1.call-start = ((), (), s32[]{:S(2)}) async-start(), calls=%async_computation.14 | async-start | bytes 3317760 | tf_op jit(solution)/shard_map/all_gather | solution.py:228
  64.0 150.8 %reduce-scatter.27.cloned.1.call-start = ((), (), s32[]{:S(2)}) async-start(), calls=%async_computation.17 | async-start | bytes 3317760 | tf_op jit(solution)/shard_map/reduce_scatter | solution.py:351
  114.9 41.7 %copy-start.8 = (f32[3,144,768]{2,1,0:T(8,128)}, f32[3,144,768]{2,1,0:T(8,128)S(1)}, u32[]{:S(2)}) copy-start(f32[3,144,768]{2,1,0:T(8,128)S(1)} %get-tuple-element.443) | copy-start | bytes 3981316
  175.0 74.9 %reduce-scatter.25.cloned.1.call-start = ((), (), s32[]{:S(2)}) async-start(), calls=%async_computation.16 | async-start | bytes 3317760 | tf_op jit(solution)/shard_map/reduce_scatter | solution.py:348
  201.5 120.8 %reduce-scatter.35.cloned.1.call-start = ((), (), s32[]{:S(2)}) async-start(), calls=%async_computation.21 | async-start | bytes 2654208 | tf_op jit(solution)/shard_map/reduce_scatter | solution.py:440
  205.3 188.6 %reduce-scatter.29.cloned.1.call-start = ((), (), s32[]{:S(2)}) async-start(), calls=%async_computation.18 | async-start | bytes 2654208 | tf_op jit(solution)/shard_map/reduce_scatter | solution.py:437
  214.7 250.9 %reduce-scatter.33.cloned.1.call-start = ((), (), s32[]{:S(2)}) async-start(), calls=%async_computation.20 | async-start | bytes 2654208 | tf_op jit(solution)/shard_map/reduce_scatter | solution.py:439
  218.1 319.1 %reduce-scatter.31.cloned.1.call-start = ((), (), s32[]{:S(2)}) async-start(), calls=%async_computation.19 | async-start | bytes 2654208 | tf_op jit(solution)/shard_map/reduce_scatter | solution.py:438
  253.2 451.2 %reduce-scatter.41.cloned.1.call-start = ((), (), s32[]{:S(2)}) async-start(), calls=%async_computation.24 | async-start | bytes 10616832 | tf_op jit(solution)/shard_map/reduce_scatter | solution.py:442
  262.4 463.7 %reduce-scatter.49.cloned.1.call-start = ((), (), s32[]{:S(2)}) async-start(), calls=%async_computation.28 | async-start | bytes 245760
  324.1 424.8 %reduce-scatter.43.cloned.1.call-start = ((), (), s32[]{:S(2)}) async-start(), calls=%async_computation.25 | async-start | bytes 245760
  395.7 520.0 %reduce-scatter.37.cloned.1.call-start = ((), (), s32[]{:S(2)}) async-start(), calls=%async_computation.22 | async-start | bytes 10616832 | tf_op jit(solution)/shard_map/reduce_scatter | solution.py:441
  404.5 535.7 %reduce-scatter.47.cloned.1.call-start = ((), (), s32[]{:S(2)}) async-start(), calls=%async_computation.27 | async-start | bytes 245760
  467.4 492.4 %reduce-scatter.45.cloned.1.call-start = ((), (), s32[]{:S(2)}) async-start(), calls=%async_computation.26 | async-start | bytes 245760
  539.0 445.2 %reduce-scatter.51.cloned.1.call-start = ((), (), s32[]{:S(2)}) async-start(), calls=%async_computation.29 | async-start | bytes 737280
  706.9 301.8 %reduce-scatter.39.cloned.1.call-start = ((), (), s32[]{:S(2)}) async-start(), calls=%async_computation.23 | async-start | bytes 737280 | tf_op jit(solution)/shard_map/reduce_scatter | solution.py:457
  754.4 163.6 %copy-start.6 = (bf16[3,128,768]{2,1,0:T(8,128)(2,1)S(1)}, bf16[3,128,768]{2,1,0:T(8,128)(2,1)}, u32[]{:S(2)}) copy-start(bf16[3,128,768]{2,1,0:T(8,128)(2,1)} %copy-done.5) | copy-start | bytes 1769476
  754.4 163.6 %copy-start.44 = (bf16[3,3,768]{2,1,0:T(4,128)(2,1)S(1)}, bf16[3,3,768]{2,1,0:T(4,128)(2,1)}, u32[]{:S(2)}) copy-start(bf16[3,3,768]{2,1,0:T(4,128)(2,1)} %copy-done.43) | copy-start | bytes 41476
  754.4 163.6 %copy-start.46 = (bf16[3,3,768]{2,1,0:T(4,128)(2,1)S(1)}, bf16[3,3,768]{2,1,0:T(4,128)(2,1)}, u32[]{:S(2)}) copy-start(bf16[3,3,768]{2,1,0:T(4,128)(2,1)} %copy-done.45) | copy-start | bytes 41476
  917.9 233.6 %all-reduce.3.cloned.1.call-start = ((), (), s32[]{:S(2)}) async-start(), calls=%async_computation.30 | async-start | bytes 335872 | tf_op jit(solution)/shard_map/psum | solution.py:464
  919.5 13.2 %collective-permute-start.4 = (bf16[3,3,768]{2,1,0:T(4,128)(2,1)S(1)}, bf16[3,3,768]{2,1,0:T(4,128)(2,1)S(1)}, u32[]{:S(2)}, u32[]{:S(2)}) collective-permute-start(bf16[3,3,768]{2,1,0:T(4,128)(2,1)S(1)} %get-tuple-element.428), channel_id=1, source_target_pairs={{1,0},{2,1},{3,2},{5,4},{6,5},{7,6},{9,8},{10,9},{11,10},{13,12},{... | collective-permute-start | bytes 41480 | tf_op jit(solution)/shard_map/ppermute | solution.py:26
  920.9 11.8 %collective-permute-start.5 = (bf16[3,3,768]{2,1,0:T(4,128)(2,1)S(1)}, bf16[3,3,768]{2,1,0:T(4,128)(2,1)S(1)}, u32[]{:S(2)}, u32[]{:S(2)}) collective-permute-start(bf16[3,3,768]{2,1,0:T(4,128)(2,1)S(1)} %get-tuple-element.429), channel_id=1, source_target_pairs={{0,1},{1,2},{2,3},{4,5},{5,6},{6,7},{8,9},{9,10},{10,11},{12,13},{... | collective-permute-start | bytes 41480 | tf_op jit(solution)/shard_map/ppermute | solution.py:24
  924.2 14.9 %collective-permute-start.6 = (bf16[3,9,768]{2,1,0:T(8,128)(2,1)S(1)}, bf16[3,9,768]{2,1,0:T(8,128)(2,1)S(1)}, u32[]{:S(2)}, u32[]{:S(2)}) collective-permute-start(bf16[3,9,768]{2,1,0:T(8,128)(2,1)S(1)} %get-tuple-element.432), channel_id=1, source_target_pairs={{1,0},{2,1},{3,2},{5,4},{6,5},{7,6},{9,8},{10,9},{11,10},{13,12},{... | collective-permute-start | bytes 124424 | tf_op jit(solution)/shard_map/ppermute | solution.py:26
  925.5 13.7 %collective-permute-start.7 = (bf16[3,9,768]{2,1,0:T(8,128)(2,1)S(1)}, bf16[3,9,768]{2,1,0:T(8,128)(2,1)S(1)}, u32[]{:S(2)}, u32[]{:S(2)}) collective-permute-start(bf16[3,9,768]{2,1,0:T(8,128)(2,1)S(1)} %get-tuple-element.433), channel_id=1, source_target_pairs={{0,1},{1,2},{2,3},{4,5},{5,6},{6,7},{8,9},{9,10},{10,11},{12,13},{... | collective-permute-start | bytes 124424 | tf_op jit(solution)/shard_map/ppermute | solution.py:24
  934.0 235.7 %copy-start.1 = (bf16[768,768]{1,0:T(8,128)(2,1)S(1)}, bf16[768,768]{1,0:T(8,128)(2,1)}, u32[]{:S(2)}) copy-start(bf16[768,768]{1,0:T(8,128)(2,1)} %param.37) | copy-start | bytes 3538948
  (92 other events, 554.7 us)
Sparse Core Ops, SparseCore 0:
  28.0 28.2 all-gather.4
  64.1 28.1 all-gather.2
  175.2 37.2 reduce-scatter.26
  215.0 34.8 reduce-scatter.24
  253.3 68.9 reduce-scatter.34
  325.6 68.1 reduce-scatter.28
  397.4 68.1 reduce-scatter.32
  469.1 68.0 reduce-scatter.30
  540.8 163.6 reduce-scatter.40
  707.3 18.7 reduce-scatter.48
  729.2 19.7 reduce-scatter.42
  752.4 163.3 reduce-scatter.36
  918.2 18.8 reduce-scatter.46
  940.0 19.7 reduce-scatter.44
  962.1 22.0 reduce-scatter.50
  986.6 22.0 reduce-scatter.38
  1016.1 135.3 all-reduce.2
where the time goes:
time: 1180 us
  waiting for transfers between devices  821 us (70%)
  matrix products  163 us (14%)
  local copies, waits for them, and re-layouts  89.6 us (8%)
  other arithmetic  65.7 us (6%)
  starting transfers between devices  21.2 us (2%)
  between operations  16.1 us (1%)
    reduce_scatter x1, waiting for transfers between devices, shards(): lax.psum_scatter(delta_up_matrix, 'page', scatter_dimension=0, tiled=True)  161 us
    psum x1, waiting for transfers between devices, shards(): lax.psum((delta_taps, delta_patch_taps, delta_query_offset, delta_value_o...  141 us
    reduce_scatter x1, waiting for transfers between devices, shards(): lax.psum_scatter(delta_down_matrix, 'page', scatter_dimension=0, tiled=True)  130 us
    unnamed x22, waiting for transfers between devices  73.3 us
    reduce_scatter x1, waiting for transfers between devices, shards(): lax.psum_scatter(delta_query_matrix, 'page', scatter_dimension=0, tiled=T...  69.7 us
    reduce_scatter x1, waiting for transfers between devices, shards(): lax.psum_scatter(delta_key_matrix, 'page', scatter_dimension=0, tiled=True)  69.1 us
    reduce_scatter x1, waiting for transfers between devices, shards(): lax.psum_scatter(delta_value_matrix, 'page', scatter_dimension=0, tiled=T...  61 us
    reduce_scatter x1, waiting for transfers between devices, shards(): lax.psum_scatter(delta_out_matrix, 'page', scatter_dimension=0, tiled=True)  59.8 us
  transfers between devices with their start and end apart: 25, of which 14 were waited for; matrix products, arithmetic and copies ran while one was open for 18% of the time, Pallas kernels for 0%

commit v1 on v0

--- a/solution.py
+++ b/solution.py
@@ -71,6 +71,63 @@
 
 def row_sum(gradient):
     return jnp.sum(gradient.astype(jnp.float32).reshape(-1, gradient.shape[-1]), axis=0)
+
+
+def swap(value, axis, bit):
+    count = lax.axis_size(axis)
+    return lax.ppermute(value, axis, [(i, i ^ bit) for i in range(count)])
+
+
+def halve(state, dim, axis, bit):
+    index = lax.axis_index(axis)
+    mine = (index // bit) % 2
+    keep = lax.dynamic_index_in_dim(state, mine, dim, keepdims=False)
+    send = lax.dynamic_index_in_dim(state, 1 - mine, dim, keepdims=False)
+    got = swap(send, axis, bit)
+    return (keep.astype(jnp.float32) + got.astype(jnp.float32)).astype(jnp.bfloat16)
+
+
+def scatter_sum(matrix, x_first):
+    pages = lax.axis_size("page")
+    rows, columns = matrix.shape
+    part = rows // pages
+    levels = pages.bit_length() - 1
+    state = matrix.reshape([2] * levels + [2, part // 2, 2, columns // 2])
+    state = halve(state, levels, "seq", 1)
+
+    def halve_x(value):
+        return halve(value, value.ndim - 2, "seq", 2)
+
+    if x_first:
+        state = halve_x(state)
+    for level in range(levels):
+        state = halve(state, levels - 1 - level, "page", 2**level)
+        if level == 0 and not x_first:
+            state = halve_x(state)
+    core = lax.axis_index("seq") % 2
+    state = state.reshape(part // 2, 2, columns // 4)
+    keep = lax.dynamic_index_in_dim(state, core, 1, keepdims=False)
+    got = swap(lax.dynamic_index_in_dim(state, 1 - core, 1, keepdims=False), "seq", 1)
+    first = jnp.where(core == 0, keep, got)
+    second = jnp.where(core == 0, got, keep)
+    return jnp.concatenate([first, second], axis=0).astype(jnp.float32)
+
+
+def total_sum(vectors):
+    flat = jnp.concatenate([vector.reshape(-1) for vector in vectors])
+    flat = jnp.pad(flat, (0, -flat.size % 1024)).reshape(-1, 128)
+    for bit in (1, 2):
+        flat = flat + swap(flat, "seq", bit)
+    bit = 1
+    while bit < lax.axis_size("page"):
+        flat = flat + swap(flat, "page", bit)
+        bit *= 2
+    flat = flat.reshape(-1)
+    result, start = [], 0
+    for vector in vectors:
+        result.append(flat[start : start + vector.size].reshape(vector.shape))
+        start += vector.size
+    return result
 
 
 def plane_hots(query_coord, key_coord, bins):
@@ -306,10 +363,7 @@
     delta_out_offset = row_sum(delta_attention)
     delta_out_matrix = outer_dot(mixture_low, delta_attention)
     delta_mixture = back_dot(delta_attention, out_weight).astype(jnp.bfloat16)
-    key_back, value_back = (
-        lax.all_gather(key_rows, "seq", axis=1, tiled=True),
-        lax.all_gather(value_rows, "seq", axis=1, tiled=True),
-    )
+    key_back, value_back = key_all, value_all
     key_back_heads = key_back.reshape(page_count, key_count, head_count, head_size)
     value_back_heads = value_back.reshape(page_count, key_count, head_count, head_size)
     weights_again = jnp.exp(attention_scores(key_back) - log_total)
@@ -433,35 +487,18 @@
     patches_gradient = delta_hidden[:, span_size:] + delta_patch_masked * patch_factor.astype(
         jnp.float32
     )
-    matrix_rows = (
-        lax.psum_scatter(delta_query_matrix, "page", scatter_dimension=0, tiled=True),
-        lax.psum_scatter(delta_key_matrix, "page", scatter_dimension=0, tiled=True),
-        lax.psum_scatter(delta_value_matrix, "page", scatter_dimension=0, tiled=True),
-        lax.psum_scatter(delta_out_matrix, "page", scatter_dimension=0, tiled=True),
-        lax.psum_scatter(delta_up_matrix, "page", scatter_dimension=0, tiled=True),
-        lax.psum_scatter(delta_down_matrix, "page", scatter_dimension=0, tiled=True),
-    )
-    matrix_parts = (
-        lax.psum_scatter(
-            matrix_rows[0].astype(jnp.bfloat16), "seq", scatter_dimension=1, tiled=True
-        ).astype(jnp.float32),
-        lax.psum_scatter(
-            matrix_rows[1].astype(jnp.bfloat16), "seq", scatter_dimension=1, tiled=True
-        ).astype(jnp.float32),
-        lax.psum_scatter(
-            matrix_rows[2].astype(jnp.bfloat16), "seq", scatter_dimension=1, tiled=True
-        ).astype(jnp.float32),
-        lax.psum_scatter(
-            matrix_rows[3].astype(jnp.bfloat16), "seq", scatter_dimension=1, tiled=True
-        ).astype(jnp.float32),
-        lax.psum_scatter(
-            matrix_rows[4].astype(jnp.bfloat16), "seq", scatter_dimension=1, tiled=True
-        ).astype(jnp.float32),
-        lax.psum_scatter(
-            matrix_rows[5].astype(jnp.bfloat16), "seq", scatter_dimension=1, tiled=True
-        ).astype(jnp.float32),
-    )
-    vector_parts = lax.psum(
+    matrix_parts = [
+        scatter_sum(matrix.astype(jnp.bfloat16), x_first)
+        for matrix, x_first in (
+            (delta_query_matrix, True),
+            (delta_key_matrix, True),
+            (delta_value_matrix, False),
+            (delta_out_matrix, False),
+            (delta_up_matrix, True),
+            (delta_down_matrix, False),
+        )
+    ]
+    vector_parts = total_sum(
         (
             delta_taps,
             delta_patch_taps,
@@ -477,8 +514,7 @@
             delta_line,
             delta_across,
             delta_upward,
-        ),
-        ("page", "seq"),
+        )
     )
     return (
         output[:, :span_size],

time: 1180 us -> 535 us (0.45)
  waiting for transfers between devices: 821 us -> 97.4 us
  local copies, waits for them, and re-layouts: 89.6 us -> 134 us
  starting transfers between devices: 21.2 us -> 54.6 us
    reduce_scatter x7 -> x0, waiting for transfers between devices: 573 us -> none  [the longest x1 161 us: shards(): lax.psum_scatter(delta_up_matrix, 'page', scatter_dimension=0, tiled=True)]
    psum x1 -> x0, waiting for transfers between devices: 141 us -> none  [shards(): lax.psum((delta_taps, delta_patch_taps, delta_query_offset, delta_value_o...]
    ppermute x0 -> x41, waiting for transfers between devices: none -> 96.7 us  [swap(): return lax.ppermute(value, axis, [(i, i ^ bit) for i in range(count)])]
    unnamed x22 -> x4, waiting for transfers between devices: 73.3 us -> 0.07 us
    reshape x0 -> x23, local copies, waits for them, and re-layouts: none -> 37.7 us  [the longest x6 29.7 us: scatter_sum(): state = matrix.reshape([2] * levels + [2, part // 2, 2, columns // 2])]
    ppermute x0 -> x41, starting transfers between devices: none -> 35.1 us  [swap(): return lax.ppermute(value, axis, [(i, i ^ bit) for i in range(count)])]
    reduce_scatter x1, waiting for transfers between devices: 31.8 us -> 0.01 us  [shards(): lax.psum_scatter(delta_key_all.astype(jnp.bfloat16), 'seq', scatter_dimen...]
    dynamic_slice x0 -> x20, local copies, waits for them, and re-layouts: none -> 28.6 us  [the longest x6 18.4 us: halve(): keep = lax.dynamic_index_in_dim(state, mine, dim, keepdims=False)]
  transfers between devices with their start and end apart: 25 -> 53, of which waited for: 14 -> 25; matrix products, arithmetic and copies ran while one was open for 18% -> 44% of each run, Pallas kernels for 0% -> 0%
where the time goes in v1:
time: 535 us; the launch traced here: 530 us
  matrix products  157 us (29%)
  local copies, waits for them, and re-layouts  134 us (25%)
  waiting for transfers between devices  97.4 us (18%)
  other arithmetic  69.9 us (13%)
  starting transfers between devices  54.6 us (10%)
  between operations  17.3 us (3%)
    ppermute x41, waiting for transfers between devices, swap(): return lax.ppermute(value, axis, [(i, i ^ bit) for i in range(count)])  96.7 us
    ppermute x41, starting transfers between devices, swap(): return lax.ppermute(value, axis, [(i, i ^ bit) for i in range(count)])  35.1 us
    reshape x6, local copies, waits for them, and re-layouts, scatter_sum(): state = matrix.reshape([2] * levels + [2, part // 2, 2, columns // 2])  29.7 us
    dot_general x6, matrix products, back_dot(): lax.dot_general(operand.reshape(-1, operand.shape[-1]), matrix, (((1,), (...  20.5 us
    dot_general x6, matrix products, outer_dot(): lax.dot_general(operand.reshape(-1, operand.shape[-1]), gradient.reshape(...  18.6 us
    dynamic_slice x6, local copies, waits for them, and re-layouts, halve(): keep = lax.dynamic_index_in_dim(state, mine, dim, keepdims=False)  18.4 us
    dot_general x1, matrix products, attention_scores(): jnp.einsum('pqhe,pkhe->phqk', query_heads, key_heads, preferred_element_t...  15.6 us
    dot_general x6, matrix products, flat_dot(): jnp.dot(operand.reshape(-1, operand.shape[-1]), matrix, preferred_element...  14.6 us
  transfers between devices with their start and end apart: 53, of which 25 were waited for; matrix products, arithmetic and copies ran while one was open for 44% of the time, Pallas kernels for 0%

profile of v1, /device:TPU:0, one launch (start us, length us, event | category | flops | bytes accessed | tf_op | source)
XLA Modules:
  0.0 529.9 jit_solution(5774401887559421802)
XLA Ops:
  28.1 34.1 %while.28 = (s32[]{:T(128)}, f32[3,12,144,576]{3,2,1,0:T(8,128)}, s32[3,2,576]{2,1,0:T(2,128)S(1)}, s32[3,2,144]{2,1,0:T(2,128)S(1)}, bf16[12,64]{1,0:T(8,128)(2...) while((s32[]{:T(128)}, f32[3,12,144,576]{3,2,1,0:T(8,128)}, ...), condition=%wide.region_1.2_spmd, body=%wide.region_0.1_spmd.sunk | while | flops 269402112 | bytes 21696516 | solution.py:315
  73.8 5.4 %copy.153 = bf16[3,576,768]{1,2,0:T(8,128)(2,1)} copy(bf16[3,576,768]{2,1,0:T(8,128)(2,1)} %all-gather.5.cloned.1.call-done) | data formatting | bytes 5308416 | tf_op jit(solution)/shard_map/all_gather | solution.py:284
  79.2 15.6 %fusion.227 = (f32[3,12,144]{2,1,0:T(8,128)S(1)}, f32[3,12,144,576]{3,2,1,0:T(8,128)}) fusion(f32[3,12,144,576]{3,2,1,0:T(8,128)} %get-tuple-element.221, f32[12,144,576]{2,1,0:T(8,128)} %copy.154, bf16[3,144,12,64]{1,3,2,0:T(8,128)(2,1)S(1)} %bitcast.500, bf16[3,576,12,64]{1,3,2,0:T(8,128)(2,1)} %bitcast.493, pred[3,576]{1,0:T(4,128)(4,1)S(1)} %broadcast_in_dim.63), kind=kOutput, calls=%fused_computation.592 | convolution fusion | flops 397130688 | bytes 31209408 | tf_op jit(solution)/shard_map/pqhe,pkhe->phqk/dot_general | solution.py:321
  94.8 6.6 %fusion.44 = f32[3,12,144]{2,1,0:T(8,128)S(1)} fusion(f32[3,12,144,576]{3,2,1,0:T(8,128)} %get-tuple-element.481, f32[3,12,144]{2,1,0:T(8,128)S(1)} %get-tuple-element.480), kind=kLoop, calls=%fused_computation.96 | loop fusion | flops 5966784 | bytes 11985408 | tf_op jit(solution)/shard_map/reduce_sum | solution.py:332
  101.5 5.4 %copy.151 = bf16[3,576,768]{1,2,0:T(8,128)(2,1)} copy(bf16[3,576,768]{2,1,0:T(8,128)(2,1)} %all-gather.3.cloned.1.call-done) | data formatting | bytes 5308416 | tf_op jit(solution)/shard_map/all_gather | solution.py:285
  106.9 7.4 %fusion.79 = bf16[3,12,64,144]{3,2,1,0:T(8,128)(2,1)S(1)} fusion(bf16[3,576,12,64]{1,3,2,0:T(8,128)(2,1)} %bitcast.496, f32[3,12,144,576]{3,2,1,0:T(8,128)} %get-tuple-element.481, f32[3,12,144]{2,1,0:T(8,128)S(1)} %fusion.44, f32[3,12,144]{2,1,0:T(8,128)S(1)} %get-tuple-element.480), kind=kOutput, calls=%fused_computation.177 | convolution fusion | flops 391495680 | bytes 15303168 | tf_op jit(solution)/shard_map/phqk,pkhe->pqhe/dot_general | solution.py:336
  115.7 6.6 %fusion.96 = (u8[144,3072]{1,0:T(8,128)(4,1)S(1)}, u8[144,3072]{1,0:T(8,128)(4,1)S(1)}, f32[3,144,3072]{2,1,0:T(8,128)S(1)}) fusion(f32[3072]{0:T(1024)S(1)} %convert_element_type.730, bf16[768,3072]{1,0:T(8,128)(2,1)} %param.38, f32[3,144,768]{2,1,0:T(8,128)S(1)} %get-tuple-element.483, f32[768]{0:T(1024)S(1)} %convert_element_type.728, ...), kind=kOutput, calls=%fused_computation.205 | convolution fusion | flops 2057785344 | bytes 12260736 | tf_op jit(solution)/shard_map/dot_general | solution.py:46
  122.3 12.4 %multiply_convert_fusion.2 = (bf16[3,144,3072]{2,1,0:T(8,128)(2,1)S(1)}, f32[3,144,3072]{2,1,0:T(8,128)S(1)}) fusion(f32[3,144,3072]{2,1,0:T(8,128)S(1)} %get-tuple-element.484, f32[3072]{0:T(1024)S(1)} %convert_element_type.730, u8[144,3072]{1,0:T(8,128)(4,1)S(1)} %get-tuple-element.325, u8[144,3072]{1,0:T(8,128)(4,1)S(1)} %get-tuple-element.324), kind=kLoop, calls=%fused_computation.116 | loop fusion | flops 94224384 | bytes 14168064 | tf_op jit(solution)/shard_map/convert_element_type | solution.py:345
  142.1 8.3 %convert_reduce_fusion.1 = (f32[3072]{0:T(1024)}, bf16[3,144,3072]{2,1,0:T(8,128)(2,1)}) fusion(f32[3,144,3072]{2,1,0:T(8,128)S(1)} %get-tuple-element.410, bf16[3,144,768]{2,1,0:T(8,128)(2,1)S(1)} %get-tuple-element.402, bf16[3072,768]{1,0:T(8,128)(2,1)} %param.39, f32[3,144,3072]{2,1,0:T(8,128)S(1)} %get-tuple-element.484, ...), kind=kOutput, calls=%fused_computation.114 | convolution fusion | flops 2060989440 | bytes 18677760 | tf_op jit(solution)/shard_map/dot_general | solution.py:54
  150.4 6.6 %multiply_reduce_fusion.1 = (f32[768]{0:T(1024)}, f32[3,144]{1,0:T(4,128)S(1)}, f32[768]{0:T(1024)}, f32[3,144,768]{2,1,0:T(8,128)S(1)}) fusion(f32[3,144,768]{2,1,0:T(8,128)S(1)} %get-tuple-element.483, f32[3,144]{1,0:T(4,128)S(1)} %fusion.197, f32[3,144]{1,0:T(4,128)S(1)} %broadcast_multiply_fusion.3, f32[768]{0:T(1024)S(1)} %convert_element_type.727, ...), kind=kOutput, calls=%fused_computation.195 | convolution fusion | flops 2045065344 | bytes 12042048 | tf_op jit(solution)/shard_map/dot_general | solution.py:54
  163.1 4.9 bitcast_convert_fusion.1
  173.8 7.4 %fusion.74 = bf16[3,12,64,576]{3,2,1,0:T(8,128)(2,1)} fusion(bf16[3,144,12,64]{1,3,2,0:T(8,128)(2,1)S(1)} %bitcast.498, f32[3,12,144,576]{3,2,1,0:T(8,128)} %get-tuple-element.481, f32[3,12,144]{2,1,0:T(8,128)S(1)} %log_add_fusion), kind=kOutput, calls=%fused_computation.163 | convolution fusion | flops 389505024 | bytes 15282432 | tf_op jit(solution)/shard_map/phqk,pqhe->pkhe/dot_general | solution.py:398
  181.2 10.8 %multiply_reduce_fusion = (f32[3,12,144]{2,1,0:T(8,128)S(1)}, f32[3,12,144,576]{3,2,1,0:T(8,128)}) fusion(f32[3,12,144,576]{3,2,1,0:T(8,128)} %get-tuple-element.481, f32[3,12,144]{2,1,0:T(8,128)S(1)} %log_add_fusion, bf16[3,144,12,64]{1,3,2,0:T(8,128)(2,1)S(1)} %bitcast.499, bf16[3,576,12,64]{1,3,2,0:T(8,128)(2,1)} %bitcast.497), kind=kOutput, calls=%fused_computation.88 | convolution fusion | flops 391158720 | bytes 27247104 | tf_op jit(solution)/shard_map/pqhe,pkhe->phqk/dot_general | solution.py:372
  192.0 10.9 %convert_reduce_fusion = (bf16[12,144,576]{2,1,0:T(8,128)(2,1)}, bf16[3,12,144,576]{3,2,1,0:T(8,128)(2,1)}) fusion(f32[3,12,144,576]{3,2,1,0:T(8,128)} %get-tuple-element.489, f32[3,12,144]{2,1,0:T(8,128)S(1)} %get-tuple-element.488, f32[3,12,144,576]{3,2,1,0:T(8,128)S(1)} %bitcast.492, f32[3,12,144]{2,1,0:T(8,128)S(1)} %log_add_fusion), kind=kLoop, calls=%fused_computation.86 | loop fusion | flops 16920576 | bytes 31891968 | tf_op jit(solution)/shard_map/aiey,jey->ij/reduce_sum | solution.py:411
  202.9 7.7 %convert_reduce_fusion.2 = (f32[12,64]{1,0:T(8,128)S(1)}, bf16[3,12,64,144]{3,2,1,0:T(8,128)(2,1)}) fusion(bf16[3,576,12,64]{1,3,2,0:T(8,128)(2,1)} %bitcast.494, bf16[3,12,144,576]{3,2,1,0:T(8,128)(2,1)} %get-tuple-element.626), kind=kOutput, calls=%fused_computation.161 | convolution fusion | flops 383532288 | bytes 9292800 | tf_op jit(solution)/shard_map/phqk,pkhe->pqhe/dot_general | solution.py:381
  221.7 11.6 %reshape.1024 = bf16[2,2,2,2,48,2,1536]{6,5,4,3,2,1,0:T(2,128)(2,1)} reshape(bf16[768,3072]{1,0:T(8,128)(2,1)} %bitcast_convert_fusion.1) | data formatting | bytes 9437184 | tf_op jit(solution)/shard_map/reshape | solution.py:95
  233.3 10.1 %reshape.1026 = bf16[2,2,2,2,192,2,384]{6,5,4,3,2,1,0:T(2,128)(2,1)} reshape(bf16[3072,768]{1,0:T(8,128)(2,1)} %bitcast_convert_fusion) | data formatting | bytes 9437184 | tf_op jit(solution)/shard_map/reshape | solution.py:95
  243.4 5.6 %constant_dynamic-slice_fusion.8 = (bf16[2,2,2,1,192,2,384]{6,5,4,3,2,1,0:T(2,128)(2,1)S(1)}, bf16[2,2,2,1,192,2,384]{6,5,4,3,2,1,0:T(2,128)(2,1)S(1)}) fusion(bf16[2,2,2,2,192,2,384]{6,5,4,3,2,1,0:T(2,128)(2,1)} %reshape.1026, s32[]{:T(128)S(6)} %select_n.448, s32[]{:T(128)S(6)} %select_n.449), kind=kLoop, calls=%fused_computation.452 | loop fusion | bytes 9437192 | tf_op jit(solution)/shard_map/jit(dynamic_index_in_dim)/dynamic_slice | solution.py:84
  250.9 5.3 %copy.160 = bf16[3,576,768]{2,1,0:T(8,128)(2,1)} copy(bf16[3,576,768]{1,2,0:T(8,128)(2,1)} %bitcast.495) | data formatting | bytes 5308416 | tf_op jit(solution)/shard_map/convert_element_type | solution.py:406
  256.3 7.0 %constant_dynamic-slice_fusion.12 = (bf16[2,2,2,1,48,2,1536]{6,5,4,3,2,1,0:T(2,128)(2,1)}, bf16[2,2,2,1,48,2,1536]{6,5,4,3,2,1,0:T(2,128)(2,1)S(1)}) fusion(bf16[2,2,2,2,48,2,1536]{6,5,4,3,2,1,0:T(2,128)(2,1)} %reshape.1024, s32[]{:T(128)S(6)} %select_n.448, s32[]{:T(128)S(6)} %select_n.449), kind=kLoop, calls=%fused_computation.456 | loop fusion | bytes 9437192 | tf_op jit(solution)/shard_map/jit(dynamic_index_in_dim)/dynamic_slice | solution.py:84
  265.6 37.6 %while.29 = (s32[]{:T(128)}, f32[3,12,64]{2,1,0:T(8,128)S(1)}, f32[3,12,64]{2,1,0:T(8,128)}, bf16[3,12,144,576]{3,2,1,0:T(8,128)(2,1)}, s32[3,2,576]{2,1,0:T(2,1...) while((s32[]{:T(128)}, f32[3,12,64]{2,1,0:T(8,128)S(1)}, f32[3,12,64]{2,1,0:T(8,128)}, ...), condition=%wide.region_26.27_spmd, body=%wide.region_25.26_spmd.sunk | while | flops 268406784 | bytes 9581581 | solution.py:427
  282.3 4.5 fusion.276
  294.8 4.5 fusion.276
  316.8 5.3 %copy.159 = bf16[3,576,768]{2,1,0:T(8,128)(2,1)} copy(bf16[3,576,768]{1,2,0:T(8,128)(2,1)} %bitcast.502) | data formatting | bytes 5308416 | tf_op jit(solution)/shard_map/convert_element_type | solution.py:403
  327.8 6.1 %collective-permute-done.27 = bf16[2,2,48,2,384]{4,2,1,0,3:T(8,128)(2,1)S(1)} collective-permute-done((bf16[2,2,48,2,384]{4,2,1,0,3:T(8,128)(2,1)S(1)}, bf16[2,2,48,2,384]{4,2,1,0,3:T(8,128)(2,1)S(1)}, u32[]{:S(2)}, u32[]{:S(2)}) %collective-permute-start.27) | collective-permute-done | bytes 294944 | tf_op jit(solution)/shard_map/ppermute | solution.py:78
  365.4 18.7 %collective-permute-done.33 = bf16[2,2,2,48,1536]{4,3,2,1,0:T(8,128)(2,1)} collective-permute-done((bf16[2,2,2,48,1536]{4,3,2,1,0:T(8,128)(2,1)S(1)}, bf16[2,2,2,48,1536]{4,3,2,1,0:T(8,128)(2,1)}, u32[]{:S(2)}, u32[]{:S(2)}) %collective-permute-start.33) | collective-permute-done | bytes 1179680 | tf_op jit(solution)/shard_map/ppermute | solution.py:78
  394.3 10.3 %collective-permute-done.34 = bf16[2,2,48,1536]{3,2,1,0:T(8,128)(2,1)S(1)} collective-permute-done((bf16[2,2,48,1536]{3,2,1,0:T(8,128)(2,1)S(1)}, bf16[2,2,48,1536]{3,2,1,0:T(8,128)(2,1)S(1)}, u32[]{:S(2)}, u32[]{:S(2)}) %collective-permute-start.34) | collective-permute-done | bytes 589856 | tf_op jit(solution)/shard_map/ppermute | solution.py:78
  409.1 5.7 %collective-permute-done.35 = bf16[2,48,1536]{2,1,0:T(8,128)(2,1)S(1)} collective-permute-done((bf16[2,48,1536]{2,1,0:T(8,128)(2,1)S(1)}, bf16[2,48,1536]{2,1,0:T(8,128)(2,1)S(1)}, u32[]{:S(2)}, u32[]{:S(2)}) %collective-permute-start.35) | collective-permute-done | bytes 294944 | tf_op jit(solution)/shard_map/ppermute | solution.py:78
  417.6 5.1 collective-permute-done.41
  424.5 6.6 %collective-permute-done.42 = bf16[192,384]{1,0:T(8,128)(2,1)S(1)} collective-permute-done((bf16[192,384]{1,0:T(8,128)(2,1)S(1)}, bf16[192,384]{1,0:T(8,128)(2,1)S(1)}, u32[]{:S(2)}, u32[]{:S(2)}) %collective-permute-start.42) | collective-permute-done | bytes 147488 | tf_op jit(solution)/shard_map/ppermute | solution.py:78
  481.8 6.3 %collective-permute-done.48 = f32[200,128]{1,0:T(8,128)S(1)} collective-permute-done((f32[200,128]{1,0:T(8,128)S(1)}, f32[200,128]{1,0:T(8,128)S(1)}, u32[]{:S(2)}, u32[]{:S(2)}) %collective-permute-start.48) | collective-permute-done | bytes 102432 | tf_op jit(solution)/shard_map/ppermute | solution.py:78
  497.2 6.4 %collective-permute-done.21 = bf16[2,2,48,2,384]{4,2,1,0,3:T(8,128)(2,1)S(1)} collective-permute-done((bf16[2,2,48,2,384]{4,2,1,0,3:T(8,128)(2,1)S(1)}, bf16[2,2,48,2,384]{4,2,1,0,3:T(8,128)(2,1)S(1)}, u32[]{:S(2)}, u32[]{:S(2)}) %collective-permute-start.21) | collective-permute-done | bytes 294944 | tf_op jit(solution)/shard_map/ppermute | solution.py:78
  (636 shorter events, 277.1 us)
Async XLA Ops:
  7.3 66.5 %all-gather.5.cloned.1.call-start = ((), (), s32[]{:S(2)}) async-start(), calls=%async_computation.3 | async-start | bytes 3317760 | tf_op jit(solution)/shard_map/all_gather | solution.py:284
  8.5 16.0 %collective-permute-start.3 = (bf16[3,9,768]{2,1,0:T(8,128)(2,1)S(1)}, bf16[3,9,768]{2,1,0:T(8,128)(2,1)S(1)}, u32[]{:S(2)}, u32[]{:S(2)}) collective-permute-start(bf16[3,9,768]{2,1,0:T(8,128)(2,1)S(1)} %get-tuple-element.466), channel_id=1, source_target_pairs={{1,0},{2,1},{3,2},{5,4},{6,5},{7,6},{9,8},{10,9},{11,10},{13,12},{... | collective-permute-start | bytes 124424 | tf_op jit(solution)/shard_map/ppermute | solution.py:26
  9.8 14.8 %collective-permute-start.2 = (bf16[3,9,768]{2,1,0:T(8,128)(2,1)S(1)}, bf16[3,9,768]{2,1,0:T(8,128)(2,1)S(1)}, u32[]{:S(2)}, u32[]{:S(2)}) collective-permute-start(bf16[3,9,768]{2,1,0:T(8,128)(2,1)S(1)} %get-tuple-element.467), channel_id=1, source_target_pairs={{0,1},{1,2},{2,3},{4,5},{5,6},{6,7},{8,9},{9,10},{10,11},{12,13},{... | collective-permute-start | bytes 124424 | tf_op jit(solution)/shard_map/ppermute | solution.py:24
  27.8 73.7 %all-gather.3.cloned.1.call-start = ((), (), s32[]{:S(2)}) async-start(), calls=%async_computation.2 | async-start | bytes 3317760 | tf_op jit(solution)/shard_map/all_gather | solution.py:285
  63.9 370.3 %reduce-scatter.5.cloned.1.call-start = ((), (), s32[]{:S(2)}) async-start(), calls=%async_computation.5 | async-start | bytes 3317760 | tf_op jit(solution)/shard_map/reduce_scatter | solution.py:405
  219.1 103.0 %collective-permute-start.26 = (bf16[2,2,2,48,2,384]{5,3,1,0,4,2:T(8,128)(2,1)}, bf16[2,2,2,48,2,384]{5,3,1,0,4,2:T(8,128)(2,1)}, u32[]{:S(2)}, u32[]{:S(2)}) collective-permute-start(bf16[2,2,2,48,2,384]{5,3,1,0,4,2:T(8,128)(2,1)} %bitcast.460), channel_id=1, source_target_pairs={{0,1},{1,0},{2,3},{3,2},{4,5},{5,4},{6,7},{7,6},{8,9},{9,8},{10,11... | collective-permute-start | bytes 1769480 | tf_op jit(solution)/shard_map/ppermute | solution.py:78
  256.2 183.1 %reduce-scatter.3.cloned.1.call-start = ((), (), s32[]{:S(2)}) async-start(), calls=%async_computation.4 | async-start | bytes 3317760 | tf_op jit(solution)/shard_map/reduce_scatter | solution.py:402
  265.1 85.9 %collective-permute-start.32 = (bf16[2,2,2,48,2,1536]{5,3,2,1,0,4:T(8,128)(2,1)}, bf16[2,2,2,48,2,1536]{5,3,2,1,0,4:T(8,128)(2,1)}, u32[]{:S(2)}, u32[]{:S(2)}) collective-permute-start(bf16[2,2,2,48,2,1536]{5,3,2,1,0,4:T(8,128)(2,1)} %bitcast.459), channel_id=1, source_target_pairs={{0,1},{1,0},{2,3},{3,2},{4,5},{5,4},{6,7},{7,6},{8,9},{9,8},{10,11... | collective-permute-start | bytes 7077896 | tf_op jit(solution)/shard_map/ppermute | solution.py:78
  265.1 96.5 %collective-permute-start.38 = (bf16[2,2,2,192,2,384]{5,3,1,0,4,2:T(8,128)(2,1)}, bf16[2,2,2,192,2,384]{5,3,1,0,4,2:T(8,128)(2,1)}, u32[]{:S(2)}, u32[]{:S(2)}) collective-permute-start(bf16[2,2,2,192,2,384]{5,3,1,0,4,2:T(8,128)(2,1)} %bitcast.458), channel_id=1, source_target_pairs={{0,1},{1,0},{2,3},{3,2},{4,5},{5,4},{6,7},{7,6},{8,9},{9,8},{10,11... | collective-permute-start | bytes 7077896 | tf_op jit(solution)/shard_map/ppermute | solution.py:78
  313.1 12.9 %collective-permute-start.8 = (bf16[2,2,2,48,2,384]{5,3,2,1,0,4:T(8,128)(2,1)}, bf16[2,2,2,48,2,384]{5,3,2,1,0,4:T(8,128)(2,1)}, u32[]{:S(2)}, u32[]{:S(2)}) collective-permute-start(bf16[2,2,2,48,2,384]{5,3,2,1,0,4:T(8,128)(2,1)} %bitcast.463), channel_id=1, source_target_pairs={{0,1},{1,0},{2,3},{3,2},{4,5},{5,4},{6,7},{7,6},{8,9},{9,8},{10,11... | collective-permute-start | bytes 1769480 | tf_op jit(solution)/shard_map/ppermute | solution.py:78
  324.4 9.5 %collective-permute-start.27 = (bf16[2,2,48,2,384]{4,2,1,0,3:T(8,128)(2,1)S(1)}, bf16[2,2,48,2,384]{4,2,1,0,3:T(8,128)(2,1)S(1)}, u32[]{:S(2)}, u32[]{:S(2)}) collective-permute-start(bf16[2,2,48,2,384]{4,2,1,0,3:T(8,128)(2,1)S(1)} %dynamic-slice_bitcast_fusion.6), channel_id=1, source_target_pairs={{0,4},{4,0},{8,12},{12,8},{16,20},{20,16},{24,28},{28,24},{1,5},{5... | collective-permute-start | bytes 884744 | tf_op jit(solution)/shard_map/ppermute | solution.py:78
  327.3 9.2 %collective-permute-start.9 = (bf16[2,2,2,48,384]{4,3,2,1,0:T(8,128)(2,1)S(1)}, bf16[2,2,2,48,384]{4,3,2,1,0:T(8,128)(2,1)S(1)}, u32[]{:S(2)}, u32[]{:S(2)}) collective-permute-start(bf16[2,2,2,48,384]{4,3,2,1,0:T(8,128)(2,1)S(1)} %dynamic-slice_bitcast_fusion.9), channel_id=1, source_target_pairs={{0,2},{1,3},{2,0},{3,1},{4,6},{5,7},{6,4},{7,5},{8,10},{9,11},{10,... | collective-permute-start | bytes 884744 | tf_op jit(solution)/shard_map/ppermute | solution.py:78
  347.7 8.4 %collective-permute-start.12 = (bf16[48,384]{1,0:T(8,128)(2,1)}, bf16[48,384]{1,0:T(8,128)(2,1)}, u32[]{:S(2)}, u32[]{:S(2)}) collective-permute-start(bf16[48,384]{1,0:T(8,128)(2,1)} %dynamic-slice_bitcast_fusion.23), channel_id=1, source_target_pairs={{0,16},{4,20},{8,24},{12,28},{16,0},{20,4},{24,8},{28,12},{1,17},{... | collective-permute-start | bytes 110600 | tf_op jit(solution)/shard_map/ppermute | solution.py:78
  351.0 9.8 %collective-permute-start.31 = (bf16[48,192]{1,0:T(8,128)(2,1)}, bf16[48,192]{1,0:T(8,128)(2,1)}, u32[]{:S(2)}, u32[]{:S(2)}) collective-permute-start(bf16[48,192]{1,0:T(8,128)(2,1)} %bitcast.465), channel_id=1, source_target_pairs={{0,1},{1,0},{2,3},{3,2},{4,5},{5,4},{6,7},{7,6},{8,9},{9,8},{10,11... | collective-permute-start | bytes 55304 | tf_op jit(solution)/shard_map/ppermute | solution.py:78
  355.5 28.6 %collective-permute-start.33 = (bf16[2,2,2,48,1536]{4,3,2,1,0:T(8,128)(2,1)S(1)}, bf16[2,2,2,48,1536]{4,3,2,1,0:T(8,128)(2,1)}, u32[]{:S(2)}, u32[]{:S(2)}) collective-permute-start(bf16[2,2,2,48,1536]{4,3,2,1,0:T(8,128)(2,1)S(1)} %dynamic-slice_bitcast_fusion.1), channel_id=1, source_target_pairs={{0,2},{1,3},{2,0},{3,1},{4,6},{5,7},{6,4},{7,5},{8,10},{9,11},{10,... | collective-permute-start | bytes 3538952 | tf_op jit(solution)/shard_map/ppermute | solution.py:78
  364.0 28.9 %collective-permute-start.39 = (bf16[2,2,192,2,384]{4,2,1,0,3:T(8,128)(2,1)S(1)}, bf16[2,2,192,2,384]{4,2,1,0,3:T(8,128)(2,1)S(1)}, u32[]{:S(2)}, u32[]{:S(2)}) collective-permute-start(bf16[2,2,192,2,384]{4,2,1,0,3:T(8,128)(2,1)S(1)} %dynamic-slice_bitcast_fusion), channel_id=1, source_target_pairs={{0,4},{4,0},{8,12},{12,8},{16,20},{20,16},{24,28},{28,24},{1,5},{5... | collective-permute-start | bytes 3538952 | tf_op jit(solution)/shard_map/ppermute | solution.py:78
  385.7 18.9 %collective-permute-start.34 = (bf16[2,2,48,1536]{3,2,1,0:T(8,128)(2,1)S(1)}, bf16[2,2,48,1536]{3,2,1,0:T(8,128)(2,1)S(1)}, u32[]{:S(2)}, u32[]{:S(2)}) collective-permute-start(bf16[2,2,48,1536]{3,2,1,0:T(8,128)(2,1)S(1)} %dynamic-slice_bitcast_fusion.3), channel_id=1, source_target_pairs={{0,4},{4,0},{8,12},{12,8},{16,20},{20,16},{24,28},{28,24},{1,5},{5... | collective-permute-start | bytes 1769480 | tf_op jit(solution)/shard_map/ppermute | solution.py:78
  393.3 13.6 %collective-permute-start.40 = (bf16[2,2,192,384]{3,2,1,0:T(8,128)(2,1)S(1)}, bf16[2,2,192,384]{3,2,1,0:T(8,128)(2,1)S(1)}, u32[]{:S(2)}, u32[]{:S(2)}) collective-permute-start(bf16[2,2,192,384]{3,2,1,0:T(8,128)(2,1)S(1)} %dynamic-slice_bitcast_fusion.2), channel_id=1, source_target_pairs={{0,2},{1,3},{2,0},{3,1},{4,6},{5,7},{6,4},{7,5},{8,10},{9,11},{10,... | collective-permute-start | bytes 1769480 | tf_op jit(solution)/shard_map/ppermute | solution.py:78
  404.8 10.0 %collective-permute-start.35 = (bf16[2,48,1536]{2,1,0:T(8,128)(2,1)S(1)}, bf16[2,48,1536]{2,1,0:T(8,128)(2,1)S(1)}, u32[]{:S(2)}, u32[]{:S(2)}) collective-permute-start(bf16[2,48,1536]{2,1,0:T(8,128)(2,1)S(1)} %dynamic-slice_bitcast_fusion.5), channel_id=1, source_target_pairs={{0,8},{4,12},{8,0},{12,4},{16,24},{20,28},{24,16},{28,20},{1,9},{5... | collective-permute-start | bytes 884744 | tf_op jit(solution)/shard_map/ppermute | solution.py:78
  407.1 15.6 %collective-permute-start.41 = (bf16[2,192,384]{2,1,0:T(8,128)(2,1)S(1)}, bf16[2,192,384]{2,1,0:T(8,128)(2,1)S(1)}, u32[]{:S(2)}, u32[]{:S(2)}) collective-permute-start(bf16[2,192,384]{2,1,0:T(8,128)(2,1)S(1)} %dynamic-slice_bitcast_fusion.4), channel_id=1, source_target_pairs={{0,8},{4,12},{8,0},{12,4},{16,24},{20,28},{24,16},{28,20},{1,9},{5... | collective-permute-start | bytes 884744 | tf_op jit(solution)/shard_map/ppermute | solution.py:78
  414.9 9.1 %collective-permute-start.36 = (bf16[48,1536]{1,0:T(8,128)(2,1)S(1)}, bf16[48,1536]{1,0:T(8,128)(2,1)S(1)}, u32[]{:S(2)}, u32[]{:S(2)}) collective-permute-start(bf16[48,1536]{1,0:T(8,128)(2,1)S(1)} %dynamic-slice_bitcast_fusion.11), channel_id=1, source_target_pairs={{0,16},{4,20},{8,24},{12,28},{16,0},{20,4},{24,8},{28,12},{1,17},{... | collective-permute-start | bytes 442376 | tf_op jit(solution)/shard_map/ppermute | solution.py:78
  422.8 8.3 %collective-permute-start.42 = (bf16[192,384]{1,0:T(8,128)(2,1)S(1)}, bf16[192,384]{1,0:T(8,128)(2,1)S(1)}, u32[]{:S(2)}, u32[]{:S(2)}) collective-permute-start(bf16[192,384]{1,0:T(8,128)(2,1)S(1)} %dynamic-slice_bitcast_fusion.10), channel_id=1, source_target_pairs={{0,16},{4,20},{8,24},{12,28},{16,0},{20,4},{24,8},{28,12},{1,17},{... | collective-permute-start | bytes 442376 | tf_op jit(solution)/shard_map/ppermute | solution.py:78
  424.4 7.6 %collective-permute-start.37 = (bf16[48,768]{1,0:T(8,128)(2,1)S(1)}, bf16[48,768]{1,0:T(8,128)(2,1)S(1)}, u32[]{:S(2)}, u32[]{:S(2)}) collective-permute-start(bf16[48,768]{1,0:T(8,128)(2,1)S(1)} %bitcast.511), channel_id=1, source_target_pairs={{0,1},{1,0},{2,3},{3,2},{4,5},{5,4},{6,7},{7,6},{8,9},{9,8},{10,11... | collective-permute-start | bytes 221192 | tf_op jit(solution)/shard_map/ppermute | solution.py:78
  439.2 54.3 %collective-permute-start.20 = (bf16[2,2,2,48,2,384]{5,3,1,0,4,2:T(8,128)(2,1)}, bf16[2,2,2,48,2,384]{5,3,1,0,4,2:T(8,128)(2,1)}, u32[]{:S(2)}, u32[]{:S(2)}) collective-permute-start(bf16[2,2,2,48,2,384]{5,3,1,0,4,2:T(8,128)(2,1)} %bitcast.461), channel_id=1, source_target_pairs={{0,1},{1,0},{2,3},{3,2},{4,5},{5,4},{6,7},{7,6},{8,9},{9,8},{10,11... | collective-permute-start | bytes 1769480 | tf_op jit(solution)/shard_map/ppermute | solution.py:78
  458.5 37.3 %collective-permute-start.14 = (bf16[2,2,2,48,2,384]{5,3,2,1,0,4:T(8,128)(2,1)}, bf16[2,2,2,48,2,384]{5,3,2,1,0,4:T(8,128)(2,1)}, u32[]{:S(2)}, u32[]{:S(2)}) collective-permute-start(bf16[2,2,2,48,2,384]{5,3,2,1,0,4:T(8,128)(2,1)} %bitcast.462), channel_id=1, source_target_pairs={{0,1},{1,0},{2,3},{3,2},{4,5},{5,4},{6,7},{7,6},{8,9},{9,8},{10,11... | collective-permute-start | bytes 1769480 | tf_op jit(solution)/shard_map/ppermute | solution.py:78
  460.3 11.2 %collective-permute-start.4 = (bf16[3,3,768]{2,1,0:T(4,128)(2,1)S(1)}, bf16[3,3,768]{2,1,0:T(4,128)(2,1)S(1)}, u32[]{:S(2)}, u32[]{:S(2)}) collective-permute-start(bf16[3,3,768]{2,1,0:T(4,128)(2,1)S(1)} %get-tuple-element.432), channel_id=1, source_target_pairs={{1,0},{2,1},{3,2},{5,4},{6,5},{7,6},{9,8},{10,9},{11,10},{13,12},{... | collective-permute-start | bytes 41480 | tf_op jit(solution)/shard_map/ppermute | solution.py:26
  461.6 12.9 %collective-permute-start.5 = (bf16[3,3,768]{2,1,0:T(4,128)(2,1)S(1)}, bf16[3,3,768]{2,1,0:T(4,128)(2,1)S(1)}, u32[]{:S(2)}, u32[]{:S(2)}) collective-permute-start(bf16[3,3,768]{2,1,0:T(4,128)(2,1)S(1)} %get-tuple-element.433), channel_id=1, source_target_pairs={{0,1},{1,2},{2,3},{4,5},{5,6},{6,7},{8,9},{9,10},{10,11},{12,13},{... | collective-permute-start | bytes 41480 | tf_op jit(solution)/shard_map/ppermute | solution.py:24
  470.1 10.7 %collective-permute-start.6 = (bf16[3,9,768]{2,1,0:T(8,128)(2,1)S(1)}, bf16[3,9,768]{2,1,0:T(8,128)(2,1)S(1)}, u32[]{:S(2)}, u32[]{:S(2)}) collective-permute-start(bf16[3,9,768]{2,1,0:T(8,128)(2,1)S(1)} %get-tuple-element.464), channel_id=1, source_target_pairs={{1,0},{2,1},{3,2},{5,4},{6,5},{7,6},{9,8},{10,9},{11,10},{13,12},{... | collective-permute-start | bytes 124424 | tf_op jit(solution)/shard_map/ppermute | solution.py:26
  471.4 9.4 %collective-permute-start.7 = (bf16[3,9,768]{2,1,0:T(8,128)(2,1)S(1)}, bf16[3,9,768]{2,1,0:T(8,128)(2,1)S(1)}, u32[]{:S(2)}, u32[]{:S(2)}) collective-permute-start(bf16[3,9,768]{2,1,0:T(8,128)(2,1)S(1)} %get-tuple-element.465), channel_id=1, source_target_pairs={{0,1},{1,2},{2,3},{4,5},{5,6},{6,7},{8,9},{9,10},{10,11},{12,13},{... | collective-permute-start | bytes 124424 | tf_op jit(solution)/shard_map/ppermute | solution.py:24
  480.0 8.1 %collective-permute-start.48 = (f32[200,128]{1,0:T(8,128)S(1)}, f32[200,128]{1,0:T(8,128)S(1)}, u32[]{:S(2)}, u32[]{:S(2)}) collective-permute-start(f32[200,128]{1,0:T(8,128)S(1)} %add.944), channel_id=1, source_target_pairs={{0,16},{4,20},{8,24},{12,28},{16,0},{20,4},{24,8},{28,12},{1,17},{... | collective-permute-start | bytes 307208 | tf_op jit(solution)/shard_map/ppermute | solution.py:78
  494.8 8.8 %collective-permute-start.21 = (bf16[2,2,48,2,384]{4,2,1,0,3:T(8,128)(2,1)S(1)}, bf16[2,2,48,2,384]{4,2,1,0,3:T(8,128)(2,1)S(1)}, u32[]{:S(2)}, u32[]{:S(2)}) collective-permute-start(bf16[2,2,48,2,384]{4,2,1,0,3:T(8,128)(2,1)S(1)} %dynamic-slice_bitcast_fusion.7), channel_id=1, source_target_pairs={{0,4},{4,0},{8,12},{12,8},{16,20},{20,16},{24,28},{28,24},{1,5},{5... | collective-permute-start | bytes 884744 | tf_op jit(solution)/shard_map/ppermute | solution.py:78
  497.1 8.8 %collective-permute-start.15 = (bf16[2,2,2,48,384]{4,3,2,1,0:T(8,128)(2,1)S(1)}, bf16[2,2,2,48,384]{4,3,2,1,0:T(8,128)(2,1)S(1)}, u32[]{:S(2)}, u32[]{:S(2)}) collective-permute-start(bf16[2,2,2,48,384]{4,3,2,1,0:T(8,128)(2,1)S(1)} %dynamic-slice_bitcast_fusion.8), channel_id=1, source_target_pairs={{0,2},{1,3},{2,0},{3,1},{4,6},{5,7},{6,4},{7,5},{8,10},{9,11},{10,... | collective-permute-start | bytes 884744 | tf_op jit(solution)/shard_map/ppermute | solution.py:78
  (144 other events, 996.9 us)
Sparse Core Ops, SparseCore 0:
  27.9 28.2 all-gather.4
  64.0 28.2 all-gather.2
  256.4 36.7 reduce-scatter.4
  322.3 35.3 reduce-scatter.2
